TPU v7x, 128 devices: a whole 4x4x4 slice. The times are simulated.
128 devices in a mesh: lat: 8 (over x, y_lo), ord: 16 (over y_hi, z, core).
Axes of the slice: x: 4, y: 4 (y_hi: 2, y_lo: 2; y = y_hi * 2 + y_lo), z: 4, core: 2. Of those that a mesh axis runs over, the one named last changes fastest.
Arguments:
- heights: bfloat16 [2048, 43200], P(('lat', 'ord')), may hold values from -1.5 to 1.5
- panels: bfloat16 [2048, 5120, 128], P('lat', 'ord'), may hold values from -0.125 to 0.125
- ord_slot: int32 [5120], replicated, may hold values from 0 to 5119, each once
- cutoffs: int32 [5120], P('ord'), may hold values from 13360 to 21599
Outputs:
- gravity: float32 [2048, 43200], P(('lat', 'ord'))
Inputs may be any that keep to these rules, and one draw needn't show every extreme that they name: `ord_slot`: a permutation of the order slots.
All inputs are finite; a program needn't handle non-finite values.
Results may differ from a plain program's by a relative error of at most 0.0039.
Values may be sent and summed in bfloat16 or wider, within the bound.
A program may use at most 192 MiB of HBM per device.

v0:
```python
import math
import jax
import jax.numpy as jnp
from jax import lax
from jax.sharding import PartitionSpec as P

LON_SLOW = 180
LON_FAST = 240
ORDERS = 5120
DEG = 128
NMAX = 21600


def slow_tables(slow):
    index = jnp.arange(slow, dtype=jnp.int32)
    phase = index[:, None] * index[None, :] % slow
    angle = 2.0 * math.pi / slow * phase.astype(jnp.float32)
    return (jnp.cos(angle), jnp.sin(angle))


def twiddle_tables(slow, fast, blocks):
    total = slow * fast
    first = jnp.arange(slow, dtype=jnp.int32)[:, None, None]
    middle = jnp.arange(fast, dtype=jnp.int32)[None, :, None]
    last = jnp.arange(blocks, dtype=jnp.int32)[None, None, :]
    phase = (middle * first + slow * middle * last) % total
    angle = 2.0 * math.pi / total * phase.astype(jnp.float32)
    return (jnp.cos(angle), jnp.sin(angle))


def forward_spectra(values, slow, fast, orders):
    count = values.shape[0]
    grid = values.reshape(count, slow, fast)
    cosine, sine = slow_tables(slow)
    first_real = jnp.einsum("raj,ak->rkj", grid, cosine, precision=lax.Precision.HIGHEST)
    first_imag = -jnp.einsum("raj,ak->rkj", grid, sine, precision=lax.Precision.HIGHEST)
    blocks = orders // slow + 1
    twist_cos, twist_sin = twiddle_tables(slow, fast, blocks)
    joined = jnp.concatenate([first_real, first_imag], 2)
    table = jnp.concatenate(
        [jnp.concatenate([twist_cos, -twist_sin], 2), jnp.concatenate([twist_sin, twist_cos], 2)], 1
    )
    second = jnp.einsum("rkj,kjq->rkq", joined, table, precision=lax.Precision.HIGHEST)
    scale_in = 1.0 / math.sqrt(slow * fast)
    spec_real = (
        second[:, :, :blocks].transpose(0, 2, 1).reshape(count, blocks * slow)[:, 1 : orders + 1]
    )
    spec_imag = (
        second[:, :, blocks:].transpose(0, 2, 1).reshape(count, blocks * slow)[:, 1 : orders + 1]
    )
    return (spec_real * scale_in, spec_imag * scale_in)


def inverse_field(full_real, full_imag, slow, fast):
    count = full_real.shape[0]
    blocks = full_real.shape[1] // slow
    grid_real = full_real.reshape(count, blocks, slow).transpose(0, 2, 1)
    grid_imag = full_imag.reshape(count, blocks, slow).transpose(0, 2, 1)
    joined = jnp.concatenate([grid_real, grid_imag], 2)
    twist_cos, twist_sin = twiddle_tables(slow, fast, blocks)
    cos_turned = twist_cos.transpose(0, 2, 1)
    sin_turned = twist_sin.transpose(0, 2, 1)
    table = jnp.concatenate(
        [
            jnp.concatenate([cos_turned, sin_turned], 2),
            jnp.concatenate([-sin_turned, cos_turned], 2),
        ],
        1,
    )
    second = jnp.einsum("rkq,kqj->rkj", joined, table, precision=lax.Precision.HIGHEST)
    cosine, sine = slow_tables(slow)
    field = jnp.einsum("rkj,ka->raj", second[:, :, :fast], cosine, precision=lax.Precision.HIGHEST)
    field = field - jnp.einsum(
        "rkj,ka->raj", second[:, :, fast:], sine, precision=lax.Precision.HIGHEST
    )
    return field.reshape(count, slow * fast)


def fold_powers(terms, factors):
    slots = terms.shape[1]
    width = terms.shape[2]
    return jnp.sum(terms.reshape(3, 2, slots, width) * factors[:, None, None, :], axis=0)


def local(heights, panels, ord_slot, cutoffs):
    lat_count = lax.axis_size("lat")
    ord_count = lax.axis_size("ord")
    level = heights.astype(jnp.float32)
    cycle_dev = level.shape[0]
    square = level * level
    powers = jnp.concatenate([level, square, square * level], 0)
    spec_real, spec_imag = forward_spectra(powers, LON_SLOW, LON_FAST, ORDERS)
    picked = jnp.stack(
        [
            spec_real[:, ord_slot].reshape(3, cycle_dev, ORDERS),
            spec_imag[:, ord_slot].reshape(3, cycle_dev, ORDERS),
        ],
        1,
    )
    picked = picked.reshape(6, cycle_dev, ORDERS).astype(jnp.bfloat16)
    sums = jnp.einsum(
        "xrk,rkn->xkn",
        lax.all_to_all(picked, "ord", split_axis=2, concat_axis=1, tiled=True),
        panels,
        preferred_element_type=jnp.float32,
    )
    stride = (NMAX - ORDERS) // DEG
    degree_int = ORDERS + jnp.arange(DEG, dtype=jnp.int32) * stride
    degree = degree_int.astype(jnp.float32)
    factors = jnp.stack(
        [
            jnp.ones_like(degree),
            (degree + 2.0) / (2.0 * NMAX),
            (degree + 2.0) * (degree + 1.0) / (6.0 * NMAX * NMAX),
        ]
    )
    keep = (degree_int[None, :] <= cutoffs[:, None]).astype(jnp.float32)
    total = lax.psum(sums, "lat")
    folded = fold_powers(total, factors)
    coeffs = (folded * keep[None]).astype(jnp.bfloat16)
    synthesis = jnp.einsum("rkn,ckn->crk", panels, coeffs, preferred_element_type=jnp.float32)
    returned = lax.all_to_all(synthesis, "ord", split_axis=1, concat_axis=2, tiled=True)
    blocks = ORDERS // LON_SLOW + 1
    target = ord_slot + 1
    full_real = (
        jnp.zeros((cycle_dev, blocks * LON_SLOW), jnp.float32).at[:, target].set(returned[0])
    )
    full_imag = (
        jnp.zeros((cycle_dev, blocks * LON_SLOW), jnp.float32).at[:, target].set(returned[1])
    )
    field = inverse_field(full_real, full_imag, LON_SLOW, LON_FAST)
    cycles_all = cycle_dev * lat_count * ord_count
    return field * math.sqrt(cycles_all / (DEG * ORDERS))


def solution(mesh):
    return jax.shard_map(
        local,
        mesh=mesh,
        in_specs=(P(("lat", "ord"), None), P("lat", "ord", None), P(), P("ord")),
        out_specs=P(("lat", "ord"), None),
        check_vma=False,
    )
```

profile of v0, /device:TPU:1, one launch (start us, length us, event | category | flops | bytes accessed | tf_op | source)
XLA Modules:
  0.0 490.3 jit_solution(14561908962304863775)
XLA Ops:
  6.5 1.8 convert_multiply_fusion.1
  8.5 3.5 pad_maximum_fusion.1
  12.1 11.4 %reshape.129 = f32[48,180,240]{2,1,0:T(8,128)} reshape(f32[48,43200]{1,0:T(8,128)} %pad_maximum_fusion.1) | data formatting | bytes 16588800 | tf_op jit(solution)/shard_map/reshape | solution.py:33
  23.5 13.3 %convolution_bitcast_fusion = f32[48,180,240]{2,1,0:T(8,128)S(1)} fusion(f32[48,180,240]{2,1,0:T(8,128)} %reshape.129), kind=kOutput, calls=%fused_computation.48 | convolution fusion | flops 4479267840 | bytes 16588800 | tf_op jit(solution)/shard_map/raj,ak->rkj/dot_general | solution.py:35
  36.8 9.9 %negate_bitcast_fusion = f32[48,180,240]{2,1,0:T(8,128)S(1)} fusion(f32[48,180,240]{2,1,0:T(8,128)S(1)} %copy-done), kind=kOutput, calls=%fused_computation.26 | convolution fusion | flops 4481341440 | bytes 16588800 | tf_op jit(solution)/shard_map/raj,ak->rkj/dot_general | solution.py:36
  46.8 7.9 %pad_maximum_fusion = f32[48,180,480]{2,1,0:T(8,128)} fusion(f32[48,180,240]{2,1,0:T(8,128)S(1)} %negate_bitcast_fusion, f32[48,180,240]{2,1,0:T(8,128)S(1)} %convolution_bitcast_fusion), kind=kLoop, calls=%fused_computation.24 | loop fusion | flops 4147200 | bytes 33177600 | tf_op jit(solution)/shard_map/concatenate | solution.py:39
  54.7 26.4 %fusion.50 = (f32[180,240,29]{1,2,0:T(8,128)}, f32[180,240,29]{1,2,0:T(8,128)}, f32[180,240,29]{1,2,0:T(8,128)}) fusion(s32[240,29]{0,1:T(8,128)S(1)} %iota_multiply_fusion.1, s32[180,240]{1,0:T(8,128)S(1)} %iota_multiply_fusion), kind=kLoop, calls=%fused_computation.59 | loop fusion | flops 12528000 | bytes 15234240 | tf_op jit(solution)/shard_map/neg | solution.py:41
  81.1 38.4 %fusion.42 = f32[48,180,58]{2,0,1:T(8,128)S(1)} fusion(f32[48,180,480]{2,1,0:T(8,128)} %pad_maximum_fusion, f32[180,240,29]{1,2,0:T(8,128)} %get-tuple-element.15, f32[180,240,29]{1,2,0:T(8,128)} %get-tuple-element.14, f32[180,240,29]{1,2,0:T(8,128)} %get-tuple-element.13), kind=kOutput, calls=%fused_computation.57 | convolution fusion | flops 2901484800 | bytes 33626880 | tf_op jit(solution)/shard_map/rkj,kjq->rkq/dot_general | solution.py:43
  119.5 4.8 slice_bitcast_fusion.1
  124.3 4.4 copy.110
  128.7 1.7 reshape.173
  130.4 2.1 slice_multiply_fusion.1
  132.5 15.1 %gather_fusion = bf16[5120,48]{1,0:T(8,128)(2,1)S(1)} fusion(bf16[48,5120]{0,1:T(8,128)(2,1)S(1)} %slice_multiply_fusion.1, s32[5120]{0:T(1024)S(1)} %get-tuple-element.19), kind=kCustom, calls=%fused_computation | custom fusion | bytes 1003520 | tf_op jit(solution)/shard_map/gather | solution.py:95
  147.6 0.6 copy.85
  148.2 4.4 copy.111
  152.6 1.7 reshape.174
  154.3 2.1 slice_multiply_fusion
  156.4 15.1 %gather_fusion.1 = bf16[5120,48]{1,0:T(8,128)(2,1)S(1)} fusion(bf16[48,5120]{0,1:T(8,128)(2,1)S(1)} %slice_multiply_fusion, s32[5120]{0:T(1024)S(1)} %get-tuple-element.19), kind=kCustom, calls=%fused_computation.1 | custom fusion | bytes 1003520 | tf_op jit(solution)/shard_map/gather | solution.py:96
  171.5 0.6 copy.88
  172.3 8.1 %copy.90 = bf16[6,16,5120]{1,0,2:T(8,128)(2,1)} copy(bf16[6,16,5120]{2,1,0:T(8,128)(2,1)S(1)} %bitcast.67) | data formatting | bytes 1966080 | tf_op jit(solution)/shard_map/convert_element_type | solution.py:100
  180.4 10.6 %reshape.179 = bf16[16,2,15360]{2,1,0:T(2,128)(2,1)S(1)} reshape(bf16[5120,6,16]{2,1,0:T(8,128)(2,1)} %bitcast.63) | data formatting | bytes 1966080
  191.1 25.5 %all_to_all.33 = bf16[16,2,15360]{2,1,0:T(2,128)(2,1)S(1)} all-to-all(bf16[16,2,15360]{2,1,0:T(2,128)(2,1)S(1)} %reshape.179), channel_id=1, replica_groups=mesh['lat'=8,'ord'=16] {'ord'}, dimensions={0} | all-to-all | bytes 1966080 | tf_op jit(solution)/shard_map/all_to_all | solution.py:103
  216.5 10.8 %reshape.180 = bf16[5120,6,16]{2,1,0:T(8,128)(2,1)} reshape(bf16[16,2,15360]{2,1,0:T(2,128)(2,1)S(1)} %all_to_all.33) | data formatting | bytes 1966080
  227.3 8.6 %copy.92 = bf16[6,16,16,320]{3,2,1,0:T(8,128)(2,1)S(1)} copy(bf16[6,16,16,320]{2,0,3,1:T(8,128)(2,1)} %bitcast.64) | data formatting | bytes 1966080 | tf_op jit(solution)/shard_map/all_to_all | solution.py:103
  236.0 1.2 copy.93
  237.2 27.0 %fusion.54 = f32[6,320,128]{2,0,1:T(8,128)S(1)} fusion(bf16[6,256,320]{1,0,2:T(8,128)(2,1)S(1)} %copy.93, bf16[256,320,128]{2,1,0:T(8,128)(2,1)} %param.5), kind=kOutput, calls=%fused_computation.63 | convolution fusion | flops 125829120 | bytes 22937600 | tf_op jit(solution)/shard_map/xrk,rkn->xkn/dot_general | solution.py:101
  264.2 1.1 copy.95
  265.6 69.9 %all-reduce.2.cloned.1.call-done = f32[3,2,320,128]{3,2,1,0:T(8,128)} async-done(((f32[3,2,320,128]{3,2,1,0:T(8,128)}), f32[3,2,320,128]{3,2,1,0:T(8,128)}) %all-reduce.2.cloned.1.call-update) | async-done | bytes 983056 | tf_op jit(solution)/shard_map/psum | solution.py:118
  335.5 1.3 multiply_reduce_fusion
  336.8 28.5 %fusion.61 = f32[2,256,320]{1,0,2:T(2,128)S(1)} fusion(bf16[256,320,128]{2,1,0:T(8,128)(2,1)} %param.5, bf16[2,320,128]{2,1,0:T(8,128)(2,1)S(1)} %multiply_convert_fusion), kind=kOutput, calls=%fused_computation.72 | convolution fusion | flops 41943040 | bytes 21790720 | tf_op jit(solution)/shard_map/rkn,ckn->crk/dot_general | solution.py:121
  365.3 1.3 copy.98
  366.6 12.4 %all-to-all-start.1 = ((f32[2,256,320]{2,0,1:T(2,128)}), f32[2,256,320]{2,0,1:T(2,128)S(1)}, u32[]{:S(2)}, u32[]{:S(2)}) async-start(f32[2,256,320]{2,0,1:T(2,128)} %copy.98), calls=%async_computation.1 | async-start | bytes 1572864 | tf_op jit(solution)/shard_map/all_to_all | solution.py:122
  379.0 26.6 %fusion.31 = (f32[180,29,240]{2,1,0:T(8,128)}, f32[180,29,240]{2,1,0:T(8,128)}, f32[180,29,240]{2,1,0:T(8,128)}) fusion(s32[29,240]{1,0:T(8,128)S(1)} %iota_multiply_fusion.2, s32[180,240]{1,0:T(8,128)S(1)} %iota_multiply_fusion), kind=kLoop, calls=%fused_computation.42 | loop fusion | flops 12528000 | bytes 15234240 | tf_op jit(solution)/shard_map/sin | solution.py:28
  406.0 2.2 copy.101
  408.3 14.0 %scatter_custom_fusion = f32[16,5220]{0,1:T(8,128)S(1)} fusion(s32[5120]{0:T(1024)S(1)} %get-tuple-element.20, f32[5120,16]{1,0:T(8,128)} %copy.101, f32[]{:T(128)} %constant.52.clone.1), kind=kCustom, calls=%fused_computation.68 | custom fusion | bytes 334592 | tf_op jit(solution)/shard_map/scatter | solution.py:126
  422.3 0.7 copy.102
  423.0 0.7 reshape.133
  423.7 2.0 copy.103
  426.0 2.2 copy.105
  428.3 14.0 %scatter_custom_fusion.1 = f32[16,5220]{0,1:T(8,128)S(1)} fusion(s32[5120]{0:T(1024)S(1)} %get-tuple-element.20, f32[5120,16]{1,0:T(8,128)} %copy.105, f32[]{:T(128)} %constant.52.clone.1), kind=kCustom, calls=%fused_computation.66 | custom fusion | bytes 334592 | tf_op jit(solution)/shard_map/scatter | solution.py:129
  442.3 0.7 copy.106
  443.1 0.7 reshape.134
  443.7 2.0 copy.107
  445.8 23.8 %fusion.39 = f32[16,180,480]{2,0,1:T(8,128)S(1)} fusion(f32[180,29,240]{2,1,0:T(8,128)} %get-tuple-element.18, f32[180,29,240]{2,1,0:T(8,128)} %get-tuple-element.17, f32[180,29,240]{2,1,0:T(8,128)} %get-tuple-element.16, f32[16,180,29]{2,0,1:T(8,128)} %bitcast.74, f32[16,180,29]{2,0,1:T(8,128)} %bitcast.73), kind=kOutput, calls=%fused_computation.56 | convolution fusion | flops 977351040 | bytes 21231360 | tf_op jit(solution)/shard_map/rkq,kqj->rkj/dot_general | solution.py:70
  469.6 1.1 fusion.108
  470.7 4.9 %fusion.35 = f32[180,16,240]{2,0,1:T(8,128)S(1)} fusion(f32[16,180,240]{2,0,1:T(8,128)S(1)} %get-tuple-element.6), kind=kOutput, calls=%fused_computation.49 | convolution fusion | flops 1493283584 | bytes 5529600 | tf_op jit(solution)/shard_map/rkj,ka->raj/dot_general | solution.py:73
  475.6 5.1 %multiply_bitcast_fusion = f32[16,180,240]{2,1,0:T(8,128)S(1)} fusion(f32[180,16,240]{2,0,1:T(8,128)S(1)} %fusion.35, f32[16,180,240]{2,0,1:T(8,128)S(1)} %get-tuple-element.5), kind=kOutput, calls=%fused_computation.53 | convolution fusion | flops 1494665984 | bytes 8294400 | tf_op jit(solution)/shard_map/rkj,ka->raj/dot_general | solution.py:72
  480.7 2.5 mul.334
  (31 shorter events, 1.2 us)
Async XLA Ops:
  6.5 1.8 copy-start.1
  6.5 328.9 %all-reduce.2.cloned.1.call-start = ((), (), s32[]{:S(2)}) async-start(), calls=%async_computation.2 | async-start | bytes 1966080 | tf_op jit(solution)/shard_map/psum | solution.py:118
  23.5 13.3 %copy-start = (f32[48,180,240]{2,1,0:T(8,128)S(1)}, f32[48,180,240]{2,1,0:T(8,128)}, u32[]{:S(2)}) copy-start(f32[48,180,240]{2,1,0:T(8,128)} %reshape.129) | copy-start | bytes 24883204
  128.7 3.8 copy-start.2
  237.2 28.3 %copy-start.3 = (s32[320]{0:T(512)S(1)}, s32[320]{0:T(512)}, u32[]{:S(2)}) copy-start(s32[320]{0:T(512)} %param.7) | copy-start | bytes 3844
  366.6 39.0 %all-to-all-start.1 = ((f32[2,256,320]{2,0,1:T(2,128)}), f32[2,256,320]{2,0,1:T(2,128)S(1)}, u32[]{:S(2)}, u32[]{:S(2)}) async-start(f32[2,256,320]{2,0,1:T(2,128)} %copy.98), calls=%async_computation.1 | async-start | bytes 1572864 | tf_op jit(solution)/shard_map/all_to_all | solution.py:122
Sparse Core Ops, SparseCore 0:
  265.5 69.8 all-reduce.1
where the time goes:
time: 497 us; the launch traced here: 490 us
  matrix products  151 us (30%)
  local copies, waits for them, and re-layouts  145 us (29%)
  other arithmetic  72.2 us (15%)
  waiting for transfers between devices  69.9 us (14%)
  blocking collectives  25.5 us (5%)
  between operations  14 us (3%)
  starting transfers between devices  12.4 us (2%)
    psum x1, waiting for transfers between devices, local(): total = lax.psum(sums, 'lat')  69.9 us
    dot_general x1, matrix products, forward_spectra(): jnp.einsum('rkj,kjq->rkq', joined, table, precision=lax.Precision.HIGHEST)  38.4 us
    scatter x4, local copies, waits for them, and re-layouts, local(): jnp.zeros((cycle_dev, blocks * LON_SLOW), jnp.float32).at[:, target]  29.5 us
    dot_general x1, matrix products, local(): jnp.einsum('rkn,ckn->crk', panels, coeffs, preferred_element_type=jnp.flo...  28.5 us
    dot_general x1, matrix products, local(): jnp.einsum('xrk,rkn->xkn', lax.all_to_all(picked, 'ord', split_axis=2, co...  27 us
    sin x1, other arithmetic, twiddle_tables(): return (jnp.cos(angle), jnp.sin(angle))  26.6 us
    neg x1, other arithmetic, forward_spectra(): -twist_sin  26.4 us
    all_to_all x1, blocking collectives, local(): lax.all_to_all(picked, 'ord', split_axis=2, concat_axis=1, tiled=True)  25.5 us
  transfers between devices with their start and end apart: 2, of which 1 were waited for; matrix products, arithmetic and copies ran while one was open for 5% of the time, Pallas kernels for 0%

commit v1 on v0

--- a/solution.py
+++ b/solution.py
@@ -100,7 +100,10 @@
     picked = picked.reshape(6, cycle_dev, ORDERS).astype(jnp.bfloat16)
     sums = jnp.einsum(
         "xrk,rkn->xkn",
-        lax.all_to_all(picked, "ord", split_axis=2, concat_axis=1, tiled=True),
+        jnp.concatenate(
+            lax.all_to_all(jnp.stack(jnp.split(picked, lax.axis_size("ord"), axis=2)), "ord", 0, 0),
+            axis=1,
+        ),
         panels,
         preferred_element_type=jnp.float32,
     )

time: 497 us -> 461 us (0.928)
  local copies, waits for them, and re-layouts: 145 us -> 108 us
    unnamed x10 -> x23, local copies, waits for them, and re-layouts: 21.4 us -> 0.81 us
    all_to_all x2 -> x0, local copies, waits for them, and re-layouts: 9.83 us -> none  [local(): lax.all_to_all(picked, 'ord', split_axis=2, concat_axis=1, tiled=True)]
    convert_element_type x1 -> x0, local copies, waits for them, and re-layouts: 8.14 us -> none  [local(): picked = picked.reshape(6, cycle_dev, ORDERS).astype(jnp.bfloat16)]
  transfers between devices with their start and end apart: 2 -> 2, of which waited for: 1 -> 1; matrix products, arithmetic and copies ran while one was open for 5% -> 6% of each run, Pallas kernels for 0% -> 0%
where the time goes in v1:
time: 461 us; the launch traced here: 455 us
  matrix products  151 us (33%)
  local copies, waits for them, and re-layouts  108 us (23%)
  other arithmetic  72.2 us (16%)
  waiting for transfers between devices  69.4 us (15%)
  blocking collectives  28.1 us (6%)
  between operations  14.1 us (3%)
  starting transfers between devices  12.4 us (3%)
    psum x1, waiting for transfers between devices, local(): total = lax.psum(sums, 'lat')  69.4 us
    dot_general x1, matrix products, forward_spectra(): jnp.einsum('rkj,kjq->rkq', joined, table, precision=lax.Precision.HIGHEST)  38.6 us
    scatter x4, local copies, waits for them, and re-layouts, local(): jnp.zeros((cycle_dev, blocks * LON_SLOW), jnp.float32).at[:, target]  29.5 us
    dot_general x1, matrix products, local(): jnp.einsum('rkn,ckn->crk', panels, coeffs, preferred_element_type=jnp.flo...  28.5 us
    all_to_all x1, blocking collectives, local(): lax.all_to_all(jnp.stack(jnp.split(picked, lax.axis_size('ord'), axis=2))...  28.1 us
    dot_general x1, matrix products, local(): jnp.einsum('xrk,rkn->xkn', jnp.concatenate(lax.all_to_all(jnp.stack(jnp.s...  26.8 us
    sin x1, other arithmetic, twiddle_tables(): return (jnp.cos(angle), jnp.sin(angle))  26.6 us
    neg x1, other arithmetic, forward_spectra(): -twist_sin  26.4 us
  transfers between devices with their start and end apart: 2, of which 1 were waited for; matrix products, arithmetic and copies ran while one was open for 6% of the time, Pallas kernels for 0%

profile of v1, /device:TPU:1, one launch (start us, length us, event | category | flops | bytes accessed | tf_op | source)
XLA Modules:
  0.0 455.1 jit_solution(12780336627268810011)
XLA Ops:
  6.5 1.8 convert_multiply_fusion.1
  8.4 0.2 convert_element_type.66
  8.5 3.5 pad_maximum_fusion.1
  12.1 11.4 %reshape.135 = f32[48,180,240]{2,1,0:T(8,128)} reshape(f32[48,43200]{1,0:T(8,128)} %pad_maximum_fusion.1) | data formatting | bytes 16588800 | tf_op jit(solution)/shard_map/reshape | solution.py:33
  23.5 13.0 %convolution_bitcast_fusion = f32[48,180,240]{2,1,0:T(8,128)S(1)} fusion(f32[48,180,240]{2,1,0:T(8,128)} %reshape.135), kind=kOutput, calls=%fused_computation.48 | convolution fusion | flops 4479267840 | bytes 16588800 | tf_op jit(solution)/shard_map/raj,ak->rkj/dot_general | solution.py:35
  36.5 10.0 %negate_bitcast_fusion = f32[48,180,240]{2,1,0:T(8,128)S(1)} fusion(f32[48,180,240]{2,1,0:T(8,128)S(1)} %copy-done), kind=kOutput, calls=%fused_computation.26 | convolution fusion | flops 4481341440 | bytes 16588800 | tf_op jit(solution)/shard_map/raj,ak->rkj/dot_general | solution.py:36
  46.5 7.9 %pad_maximum_fusion = f32[48,180,480]{2,1,0:T(8,128)} fusion(f32[48,180,240]{2,1,0:T(8,128)S(1)} %negate_bitcast_fusion, f32[48,180,240]{2,1,0:T(8,128)S(1)} %convolution_bitcast_fusion), kind=kLoop, calls=%fused_computation.24 | loop fusion | flops 4147200 | bytes 33177600 | tf_op jit(solution)/shard_map/concatenate | solution.py:39
  54.4 26.4 %fusion.50 = (f32[180,240,29]{1,2,0:T(8,128)}, f32[180,240,29]{1,2,0:T(8,128)}, f32[180,240,29]{1,2,0:T(8,128)}) fusion(s32[240,29]{0,1:T(8,128)S(1)} %iota_multiply_fusion.1, s32[180,240]{1,0:T(8,128)S(1)} %iota_multiply_fusion), kind=kLoop, calls=%fused_computation.59 | loop fusion | flops 12528000 | bytes 15234240 | tf_op jit(solution)/shard_map/neg | solution.py:41
  80.8 38.6 %fusion.42 = f32[48,180,58]{2,0,1:T(8,128)S(1)} fusion(f32[48,180,480]{2,1,0:T(8,128)} %pad_maximum_fusion, f32[180,240,29]{1,2,0:T(8,128)} %get-tuple-element.15, f32[180,240,29]{1,2,0:T(8,128)} %get-tuple-element.14, f32[180,240,29]{1,2,0:T(8,128)} %get-tuple-element.13), kind=kOutput, calls=%fused_computation.57 | convolution fusion | flops 2901484800 | bytes 33626880 | tf_op jit(solution)/shard_map/rkj,kjq->rkq/dot_general | solution.py:43
  119.5 4.8 %slice_bitcast_fusion.1 = (f32[48,29,180]{1,0,2:T(8,128)}, f32[48,29,180]{1,0,2:T(8,128)}) fusion(f32[48,180,58]{2,0,1:T(8,128)S(1)} %fusion.42), kind=kLoop, calls=%fused_computation.47 | loop fusion | bytes 4008960 | tf_op jit(solution)/shard_map/transpose | solution.py:46
  124.2 4.4 copy.122
  128.6 1.7 reshape.181
  130.3 2.1 slice_multiply_fusion.1
  132.5 15.1 %gather_fusion = bf16[5120,48]{1,0:T(8,128)(2,1)S(1)} fusion(bf16[48,5120]{0,1:T(8,128)(2,1)S(1)} %slice_multiply_fusion.1, s32[5120]{0:T(1024)S(1)} %get-tuple-element.19), kind=kCustom, calls=%fused_computation | custom fusion | bytes 1003520 | tf_op jit(solution)/shard_map/gather | solution.py:95
  147.6 0.6 copy.99
  148.2 4.4 copy.123
  152.6 1.7 reshape.182
  154.3 2.1 slice_multiply_fusion
  156.4 15.1 %gather_fusion.1 = bf16[5120,48]{1,0:T(8,128)(2,1)S(1)} fusion(bf16[48,5120]{0,1:T(8,128)(2,1)S(1)} %slice_multiply_fusion, s32[5120]{0:T(1024)S(1)} %get-tuple-element.19), kind=kCustom, calls=%fused_computation.1 | custom fusion | bytes 1003520 | tf_op jit(solution)/shard_map/gather | solution.py:96
  171.5 0.6 copy.102
  173.2 28.1 %all_to_all.20 = bf16[16,6,16,320]{3,2,1,0:T(8,128)(2,1)S(1)} all-to-all(bf16[16,6,16,320]{3,2,1,0:T(8,128)(2,1)S(1)} %fusion.92), channel_id=1, replica_groups=mesh['lat'=8,'ord'=16] {'ord'}, dimensions={0} | all-to-all | bytes 1966080 | tf_op jit(solution)/shard_map/all_to_all | solution.py:104
  201.5 1.2 copy.105
  202.7 26.8 %fusion.54 = f32[6,320,128]{2,0,1:T(8,128)S(1)} fusion(bf16[6,256,320]{1,0,2:T(8,128)(2,1)S(1)} %copy.105, bf16[256,320,128]{2,1,0:T(8,128)(2,1)} %param.5), kind=kOutput, calls=%fused_computation.63 | convolution fusion | flops 125829120 | bytes 22937600 | tf_op jit(solution)/shard_map/xrk,rkn->xkn/dot_general | solution.py:101
  229.5 1.1 copy.107
  230.8 69.4 %all-reduce.2.cloned.1.call-done = f32[3,2,320,128]{3,2,1,0:T(8,128)} async-done(((f32[3,2,320,128]{3,2,1,0:T(8,128)}), f32[3,2,320,128]{3,2,1,0:T(8,128)}) %all-reduce.2.cloned.1.call-update) | async-done | bytes 983056 | tf_op jit(solution)/shard_map/psum | solution.py:121
  300.2 1.3 multiply_reduce_fusion
  301.6 28.5 %fusion.61 = f32[2,256,320]{1,0,2:T(2,128)S(1)} fusion(bf16[256,320,128]{2,1,0:T(8,128)(2,1)} %param.5, bf16[2,320,128]{2,1,0:T(8,128)(2,1)S(1)} %multiply_convert_fusion), kind=kOutput, calls=%fused_computation.72 | convolution fusion | flops 41943040 | bytes 21790720 | tf_op jit(solution)/shard_map/rkn,ckn->crk/dot_general | solution.py:124
  330.0 1.3 copy.110
  331.4 12.4 %all-to-all-start.1 = ((f32[2,256,320]{2,0,1:T(2,128)}), f32[2,256,320]{2,0,1:T(2,128)S(1)}, u32[]{:S(2)}, u32[]{:S(2)}) async-start(f32[2,256,320]{2,0,1:T(2,128)} %copy.110), calls=%async_computation.1 | async-start | bytes 1572864 | tf_op jit(solution)/shard_map/all_to_all | solution.py:125
  343.8 26.6 %fusion.31 = (f32[180,29,240]{2,1,0:T(8,128)}, f32[180,29,240]{2,1,0:T(8,128)}, f32[180,29,240]{2,1,0:T(8,128)}) fusion(s32[29,240]{1,0:T(8,128)S(1)} %iota_multiply_fusion.2, s32[180,240]{1,0:T(8,128)S(1)} %iota_multiply_fusion), kind=kLoop, calls=%fused_computation.42 | loop fusion | flops 12528000 | bytes 15234240 | tf_op jit(solution)/shard_map/sin | solution.py:28
  370.5 0.1 copy.112
  370.6 0.1 reshape.160
  370.8 2.2 copy.113
  373.0 14.0 %scatter_custom_fusion = f32[16,5220]{0,1:T(8,128)S(1)} fusion(s32[5120]{0:T(1024)S(1)} %get-tuple-element.20, f32[5120,16]{1,0:T(8,128)} %copy.113, f32[]{:T(128)} %constant.52.clone.1), kind=kCustom, calls=%fused_computation.68 | custom fusion | bytes 334592 | tf_op jit(solution)/shard_map/scatter | solution.py:129
  387.1 0.7 copy.114
  387.8 0.7 reshape.141
  388.5 2.0 copy.115
  390.6 0.1 reshape.168
  390.8 2.2 copy.117
  393.0 14.0 %scatter_custom_fusion.1 = f32[16,5220]{0,1:T(8,128)S(1)} fusion(s32[5120]{0:T(1024)S(1)} %get-tuple-element.20, f32[5120,16]{1,0:T(8,128)} %copy.117, f32[]{:T(128)} %constant.52.clone.1), kind=kCustom, calls=%fused_computation.66 | custom fusion | bytes 334592 | tf_op jit(solution)/shard_map/scatter | solution.py:132
  407.1 0.7 copy.118
  407.8 0.7 reshape.142
  408.5 2.0 copy.119
  410.5 23.8 %fusion.39 = f32[16,180,480]{2,0,1:T(8,128)S(1)} fusion(f32[180,29,240]{2,1,0:T(8,128)} %get-tuple-element.18, f32[180,29,240]{2,1,0:T(8,128)} %get-tuple-element.17, f32[180,29,240]{2,1,0:T(8,128)} %get-tuple-element.16, f32[16,180,29]{2,0,1:T(8,128)} %bitcast.147, f32[16,180,29]{2,0,1:T(8,128)} %bitcast.146), kind=kOutput, calls=%fused_computation.56 | convolution fusion | flops 977351040 | bytes 21231360 | tf_op jit(solution)/shard_map/rkq,kqj->rkj/dot_general | solution.py:70
  434.4 1.1 fusion.124
  435.4 4.9 %fusion.35 = f32[180,16,240]{2,0,1:T(8,128)S(1)} fusion(f32[16,180,240]{2,0,1:T(8,128)S(1)} %get-tuple-element.6), kind=kOutput, calls=%fused_computation.49 | convolution fusion | flops 1493283584 | bytes 5529600 | tf_op jit(solution)/shard_map/rkj,ka->raj/dot_general | solution.py:73
  440.4 5.1 %multiply_bitcast_fusion = f32[16,180,240]{2,1,0:T(8,128)S(1)} fusion(f32[180,16,240]{2,0,1:T(8,128)S(1)} %fusion.35, f32[16,180,240]{2,0,1:T(8,128)S(1)} %get-tuple-element.5), kind=kOutput, calls=%fused_computation.53 | convolution fusion | flops 1494665984 | bytes 8294400 | tf_op jit(solution)/shard_map/rkj,ka->raj/dot_general | solution.py:72
  445.5 2.5 mul.334
  (44 shorter events, 1.7 us)
Async XLA Ops:
  6.5 1.8 copy-start.1
  6.5 293.7 %all-reduce.2.cloned.1.call-start = ((), (), s32[]{:S(2)}) async-start(), calls=%async_computation.2 | async-start | bytes 1966080 | tf_op jit(solution)/shard_map/psum | solution.py:121
  23.5 13.0 %copy-start = (f32[48,180,240]{2,1,0:T(8,128)S(1)}, f32[48,180,240]{2,1,0:T(8,128)}, u32[]{:S(2)}) copy-start(f32[48,180,240]{2,1,0:T(8,128)} %reshape.135) | copy-start | bytes 24883204
  130.3 2.1 copy-start.2
  229.5 1.2 copy-start.3
  331.4 39.0 %all-to-all-start.1 = ((f32[2,256,320]{2,0,1:T(2,128)}), f32[2,256,320]{2,0,1:T(2,128)S(1)}, u32[]{:S(2)}, u32[]{:S(2)}) async-start(f32[2,256,320]{2,0,1:T(2,128)} %copy.110), calls=%async_computation.1 | async-start | bytes 1572864 | tf_op jit(solution)/shard_map/all_to_all | solution.py:125
Sparse Core Ops, SparseCore 0:
  230.8 69.3 all-reduce.1
